TPU v7x, 128 devices: a whole 4x4x4 slice. The times are simulated.
128 devices in a mesh: leaf: 64 (over x, y, z), rhs: 2 (over core).
Axes of the slice: x: 4, y: 4, z: 4, core: 2. Of those that a mesh axis runs over, the one named last changes fastest.
Arguments:
- points: float32 [524288, 64], P('leaf', 'rhs'), may hold values from -6 to 6
- vectors: float32 [524288, 64], P('leaf', 'rhs'), may hold values from -6 to 6
- leaf_basis: float32 [524288, 64], P('leaf'), may hold values from -0.375 to 0.375
- skel_lv0: float32 [131072, 64], P('leaf'), may hold values from -5 to 5
- skel_lv1: float32 [65536, 64], P('leaf'), may hold values from -5 to 5
- skel_lv2: float32 [32768, 64], P('leaf'), may hold values from -5 to 5
- transfer_lv1: float32 [131072, 64], P('leaf'), may hold values from -0.5 to 0.5
- transfer_lv2: float32 [65536, 64], P('leaf'), may hold values from -0.5 to 0.5
- transfer_root: float32 [32768, 64], P('leaf'), may hold values from -0.25 to 0.25
- root_skeleton_points: float32 [4096, 64], replicated, may hold values from -5 to 5
- near_mask: int32 [2048, 8], P('leaf'), may hold values from 0 to 1, as said below
- far_lv0: int32 [2048, 4], P('leaf'), may hold values 0 or 1
- far_lv1: int32 [1024, 4], P('leaf'), may hold values 0 or 1
- far_lv2: int32 [512, 4], P('leaf'), may hold values 0 or 1
Outputs:
- product: float32 [524288, 64], P('leaf', 'rhs')
Inputs may be any that keep to these rules, and one draw needn't show every extreme that they name: `near_mask`: Symmetric: the entry of leaf i at offset +d equals the entry of leaf i + d at offset -d; entries whose partner lies outside the 2048 leaves are 0.
All inputs are finite; a program needn't handle non-finite values. No bound on the sum of `far_lv0` or of `far_lv1` or of `far_lv2` on one device may be relied on, other than what follows from the above.
Results may differ from a plain program's by a relative error of at most 0.0003.
Values sent between devices are 32-bit elements; how exact they have to be, the bound alone decides.
No kernel may reach another device: no remote copies, remote signals or barrier semaphores. Data moves between devices by JAX's collectives and lax.ppermute only.
A program may use at most 128 MiB of HBM per device.

v0:
```python
import math

import jax
import jax.numpy as jnp
from jax import lax
from jax.experimental import pallas as pl
from jax.experimental.pallas import tpu as pltpu
from jax.sharding import PartitionSpec as P

DIM = 64
RANK = 64
LEAF = 256
REACH = 4
FREACH = 2
LEAVES_DEV = 32
RHS_DEV = 32
CHIPS = 64

HALF = LEAVES_DEV // 2
WINDOW = HALF + 2 * REACH
HALO = REACH * LEAF
EDGE = FREACH * RANK
LANES = LEAVES_DEV * LEAF
NEAR_OUT = HALF * LEAF + 3 * EDGE
CUT_AT = HALF * LEAF // 2
GROUP = 32
REST = 8
SCALE = math.sqrt(2.0 / 24.0 * math.log2(math.e))
CUT = -32768.0

F32 = jnp.float32
BF16 = jnp.bfloat16

NN = (((1,), (0,)), ((), ()))
NT = (((1,), (1,)), ((), ()))


def mul(left, right, dims=NN):
    return lax.dot_general(left, right, dims, preferred_element_type=F32)


def split(x):
    high = x.astype(BF16)
    return high, (x - high.astype(F32)).astype(BF16)


def mul3(left, right, dims=NN):
    rows = left.shape[0]
    left_high, left_low = split(left)
    right_high, right_low = split(right)
    both = mul(jnp.concatenate([left_high, left_low], 0), right_high, dims)
    return both[:rows] + both[rows:] + mul(left_high, right_low, dims)


def augment(points, source_extra=None, target_extra=None):
    high, low = split(points * SCALE)
    high_f, low_f = high.astype(F32), low.astype(F32)
    norm = 0.5 * jnp.sum(high_f * (high_f + 2.0 * low_f), axis=0, keepdims=True)
    first = norm.astype(BF16).astype(F32)
    second = (norm - first).astype(BF16).astype(F32)
    third = (norm - first - second).astype(BF16).astype(F32)
    width = points.shape[1]
    row = lax.broadcasted_iota(jnp.int32, (8, width), 0)

    def rows_of(start, ones):
        picked = jnp.where(row == start, -first, 0.0)
        picked = jnp.where(row == start + 1, -second, picked)
        picked = jnp.where(row == start + 2, -third, picked)
        return jnp.where((row >= ones) & (row < ones + 3), 1.0, picked)

    nothing = jnp.zeros((8, width), F32)
    rest = jnp.zeros((DIM - 16, width), BF16)

    def block(start, ones, extra):
        tail = jnp.concatenate([rows_of(start, ones), nothing if extra is None else extra], 0)
        return tail.astype(BF16), rest

    source = jnp.concatenate([high, low, high, *block(0, 3, source_extra)], 0)
    target = jnp.concatenate([high, high, low, *block(3, 0, target_extra)], 0)
    return source, target


def weights(exponent):
    return split(jnp.exp2(exponent))


def fetch(jobs, sems):
    return [pltpu.make_async_copy(src, dst, sems.at[k]) for k, (src, dst) in enumerate(jobs)]


def edge_lanes(last, width, size):
    return pl.ds(pl.multiple_of(jnp.where(last, width - size, 0), size), size)


def up_kernel(
    vec, basis, lv1, lv2, root, pts, s0, s1, s2,
    c0, c1, c2, blocks, near_msg, cross_msg,
    vec_v, basis_v, lv1_v, lv2_v, root_v, coeff0, coeff1, coeff2, top_v, near_v, cross_v, sems, out_sems,
):
    core = lax.axis_index("rhs")
    near_last, cross_last = core == 0, core == 1
    jobs = []
    for chunk in range(2):
        lanes = pl.ds(chunk * 4096, 4096)
        jobs.append((vec.at[:, lanes], vec_v.at[:, lanes]))
        jobs.append((basis.at[:, lanes], basis_v.at[:, lanes]))
    jobs += [(lv1, lv1_v), (lv2, lv2_v), (root, root_v)]
    for place, skel in enumerate((s0, s1, s2)):
        lanes = edge_lanes(near_last, skel.shape[1], EDGE)
        jobs.append((skel.at[:, lanes], near_v.at[:, pl.ds(HALO + (2 + place) * EDGE, EDGE)]))
    for msg, last in ((near_v, near_last), (cross_v, cross_last)):
        for part, array in enumerate((pts, vec)):
            lanes = edge_lanes(last, LANES, HALO)
            jobs.append((array.at[:, lanes], msg.at[pl.ds(part * 32, 32), pl.ds(0, HALO)]))
    copies = fetch(jobs, sems)
    for copy in copies:
        copy.start()

    for chunk in range(2):
        copies[2 * chunk].wait()
        copies[2 * chunk + 1].wait()
        for pair in range(8 * chunk, 8 * chunk + 8):
            parts = []
            for side in range(2):
                lanes = slice((2 * pair + side) * LEAF, (2 * pair + side + 1) * LEAF)
                parts.append(mul3(vec_v[:, lanes], basis_v[:, lanes], NT))
            coeff0[:, pair * 128 : (pair + 1) * 128] = jnp.concatenate(parts, 1)

    def up_level(children, transfer, parents, count):
        for pair in range(count // 2):
            parts = []
            for side in range(2):
                lanes = slice((2 * pair + side) * 128, (2 * pair + side + 1) * 128)
                parts.append(mul3(children[:, lanes], transfer[:, lanes], NT))
            parents[:, pair * 128 : (pair + 1) * 128] = jnp.concatenate(parts, 1)

    for copy in copies[7:]:
        copy.wait()
    body, ends_at, skel_at = pl.ds(0, HALO), pl.ds(HALO, 2 * EDGE), pl.ds(HALO + 2 * EDGE, 3 * EDGE)
    stores = fetch(
        [
            (near_v.at[:, body], near_msg.at[:, body]), (cross_v.at[:, body], cross_msg.at[:, body]),
            (near_v.at[:, skel_at], near_msg.at[:, skel_at]), (coeff0, c0), (coeff1, c1), (coeff2, c2),
            (near_v.at[:, ends_at], near_msg.at[:, ends_at]),
            (cross_v.at[:, ends_at], cross_msg.at[:, ends_at]), (top_v, blocks),
        ],
        out_sems,
    )
    for store in stores[:4]:
        store.start()
    copies[4].wait()
    up_level(coeff0, lv1_v, coeff1, LEAVES_DEV // 2)
    copies[5].wait()
    up_level(coeff1, lv2_v, coeff2, LEAVES_DEV // 4)
    for msg, last in ((near_v, near_last), (cross_v, cross_last)):
        ends = [
            jnp.where(last, ref[:, ref.shape[1] - EDGE :], ref[:, :EDGE]) for ref in (coeff0, coeff1, coeff2)
        ]
        msg[:RHS_DEV, HALO : HALO + EDGE] = ends[0]
        msg[RHS_DEV:, HALO : HALO + EDGE] = ends[1]
        msg[:RHS_DEV, HALO + EDGE : HALO + 2 * EDGE] = ends[2]
        msg[RHS_DEV:, HALO + EDGE : HALO + 2 * EDGE] = jnp.zeros((RHS_DEV, EDGE), F32)
    for store in stores[4:8]:
        store.start()
    copies[6].wait()
    top = mul3(coeff2[...], root_v[...], NT)
    packed = jnp.concatenate([top[: RHS_DEV // 2], top[RHS_DEV // 2 :]], 1)
    top_v[...] = jnp.broadcast_to(packed[None], (CHIPS, RHS_DEV // 2, 2 * RANK))
    stores[8].start()
    for store in stores:
        store.wait()


def edge_penalty(mask, core):
    count = mask.shape[1]
    first = core == 0
    linked = [
        [jnp.where(first, mask[0, 0], mask[3, count - 2]), jnp.where(first, 0, mask[2, count - 1])],
        [jnp.where(first, mask[1, 0], 0), jnp.where(first, mask[0, 1], mask[3, count - 1])],
    ]
    row = lax.broadcasted_iota(jnp.int32, (8, EDGE), 0)
    cluster = lax.broadcasted_iota(jnp.int32, (8, EDGE), 1) // RANK
    penalty = jnp.zeros((8, EDGE), F32)
    for source in range(2):
        for target in range(2):
            value = jnp.where(linked[source][target] > 0, 0.0, CUT)
            penalty = jnp.where((row == source) & (cluster == target), value, penalty)
    return penalty


def near_kernel(
    mask_any, m0_any, m1_any, m2_any, s0, s1_any, s2_any, c1_any, c2_any, own_pts, own_vec, other_pts, other_vec,
    near_msg, cross_msg, own_any, first_any, rest_any, f1_any, f2_any,
    own_out, other_out, f1, f2, m1_v, m2_v, s1, s2, c1, c2, win_pts, win_vec, source, target, vec_t, mask, m0, m1, m2, skel_own, skel_halo,
    ends_own, ends_other, pairs, sems, out_sems,
):
    core = lax.axis_index("rhs")
    body_lanes = (WINDOW - REACH) * LEAF
    main_from = pl.multiple_of(core * (LANES - body_lanes), HALO)
    main_to = pl.multiple_of((1 - core) * HALO, HALO)
    halo_to = pl.multiple_of(core * body_lanes, HALO)
    jobs = [(mask_any, mask), (m0_any, m0), (m1_any, m1), (m2_any, m2)]
    jobs += [(m1_any, m1_v), (s1_any, s1), (c1_any, c1), (m2_any, m2_v), (s2_any, s2), (c2_any, c2)]
    for half, (pts, vecs, halo) in enumerate(
        ((own_pts, own_vec, near_msg), (other_pts, other_vec, cross_msg))
    ):
        rows = pl.ds(half * 32, 32)
        main = pl.ds(main_to, body_lanes)
        edge = pl.ds(halo_to, HALO)
        jobs.append((pts.at[:, pl.ds(main_from, body_lanes)], win_pts.at[rows, main]))
        jobs.append((vecs.at[:, pl.ds(main_from, body_lanes)], win_vec.at[rows, main]))
        jobs.append((halo.at[pl.ds(0, 32), pl.ds(0, HALO)], win_pts.at[rows, edge]))
        jobs.append((halo.at[pl.ds(32, 32), pl.ds(0, HALO)], win_vec.at[rows, edge]))
    ends_at = pl.ds(HALO, 2 * EDGE)
    jobs += [(near_msg.at[:, ends_at], ends_own), (cross_msg.at[:, ends_at], ends_other)]
    jobs.append((near_msg.at[:, pl.ds(HALO + 2 * EDGE, 3 * EDGE)], skel_halo))
    for place, skel in enumerate((s0, s1_any, s2_any)):
        lanes = edge_lanes(core == 1, skel.shape[1], EDGE)
        jobs.append((skel.at[:, lanes], skel_own.at[:, pl.ds(place * EDGE, EDGE)]))
    copies = fetch(jobs, sems)
    for copy in copies:
        copy.start()

    own_out[:, : LANES // 2] = jnp.zeros((32, LANES // 2), F32)
    other_out[:, : LANES // 2] = jnp.zeros((32, LANES // 2), F32)

    copies[0].wait()
    count = jnp.int32(0)
    for leaf in range(HALF):
        for offset in range(-REACH, REACH + 1):
            pairs[count] = (leaf + REACH + offset) * 32 + leaf
            if offset == 0:
                count = count + 1
            else:
                column = REACH + offset if offset < 0 else REACH + offset - 1
                count = count + mask[column, core * HALF + leaf]
    for extra in range(REST):
        pairs[count + extra] = WINDOW * 32

    source[WINDOW] = jnp.zeros((4 * DIM, LEAF), BF16).reshape(LEAF, 4 * DIM)
    vec_t[WINDOW] = jnp.zeros((2 * 64, LEAF), BF16)

    for copy in copies[4:10]:
        copy.wait()
    couple_level(m2_v, s2, c2, f2)
    couple_level(m1_v, s1, c1, f1)
    stores = fetch(
        [
            (f1, f1_any), (f2, f2_any), (own_out, own_any), (other_out.at[:, pl.ds(0, CUT_AT)], first_any),
            (other_out.at[:, pl.ds(CUT_AT, NEAR_OUT - CUT_AT)], rest_any),
        ],
        out_sems,
    )
    for store in stores[:2]:
        store.start()
    for copy in copies[1:4] + copies[10:]:
        copy.wait()

    for leaf in range(WINDOW):
        lanes = slice(leaf * LEAF, (leaf + 1) * LEAF)
        from_side, to_side = augment(win_pts[:, lanes])
        source[leaf] = from_side.T
        if REACH <= leaf < WINDOW - REACH:
            target[leaf - REACH] = to_side
        vec_t[leaf] = jnp.concatenate(split(win_vec[:, lanes]), 0)

    row = lax.broadcasted_iota(jnp.int32, (8, EDGE), 0)
    indicator = jnp.where(row == lax.broadcasted_iota(jnp.int32, (8, EDGE), 1) // RANK, 1.0, 0.0)
    for place, far_mask in enumerate((m0, m1, m2)):
        lanes = slice(place * EDGE, (place + 1) * EDGE)
        from_side, _ = augment(skel_halo[:, lanes], indicator, None)
        _, to_side = augment(skel_own[:, lanes], None, edge_penalty(far_mask, core))
        high, low = weights(mul(from_side.T, to_side))
        rows = slice(place % 2 * 32, place % 2 * 32 + 32)
        at = slice(place // 2 * EDGE, (place // 2 + 1) * EDGE)
        cof_high, cof_low = split(jnp.concatenate([ends_own[rows, at], ends_other[rows, at]], 0))
        both = mul(jnp.concatenate([cof_high, cof_low], 0), high)
        term = both[:64] + both[64:] + mul(cof_high, low)
        lanes = slice(LANES // 2 + place * EDGE, LANES // 2 + (place + 1) * EDGE)
        own_out[:, lanes] = term[:32]
        other_out[:, lanes] = term[32:]

    def steps(start, size, number):
        def step(index, carry):
            found = []
            for k in range(size):
                code = pairs[start + index * size + k]
                src, tgt = lax.shift_right_logical(code, 5), lax.bitwise_and(code, 31)
                high, low = weights(mul(source[src], target[tgt]))
                both = mul(vec_t[src], high)
                found.append((tgt, both[:64] + both[64:] + mul(vec_t[src, :64], low)))
            for tgt, term in found:
                lanes = pl.ds(pl.multiple_of(tgt * LEAF, LEAF), LEAF)
                own_out[:, lanes] += term[:32]
                other_out[:, lanes] += term[32:]
            return carry

        lax.fori_loop(0, number, step, 0)

    full = count // GROUP
    steps(0, GROUP, full)
    steps(full * GROUP, REST, (count - full * GROUP + REST - 1) // REST)
    for store in stores[2:]:
        store.start()
    for store in stores:
        store.wait()


def couple_level(mask, skel, coeff, out):
    width = skel.shape[1]
    count = width // RANK
    cluster = lax.broadcasted_iota(jnp.int32, (count, width), 0)
    owner = lax.broadcasted_iota(jnp.int32, (count, width), 1) // RANK
    spread = jnp.where(cluster == owner, 1.0, 0.0).astype(BF16)
    allowed = mul(mask[...].astype(F32).astype(BF16), spread)
    row = lax.broadcasted_iota(jnp.int32, (8, width), 0)
    owner = lax.broadcasted_iota(jnp.int32, (8, width), 1) // RANK
    penalty = jnp.full((8, width), CUT, F32)
    for column, offset in enumerate((-2, -1, 1, 2)):
        linked = (row == lax.bitwise_and(owner + offset, 7)) & (allowed[column : column + 1] > 0.5)
        penalty = jnp.where(linked, 0.0, penalty)
    target = augment(skel[...], None, penalty)[1]

    wide = width + 2 * EDGE
    row = lax.broadcasted_iota(jnp.int32, (8, wide), 0)
    owner = lax.broadcasted_iota(jnp.int32, (8, wide), 1) // RANK - FREACH
    indicator = jnp.where(row == lax.bitwise_and(owner, 7), 1.0, 0.0)
    gap = jnp.zeros((DIM, EDGE), F32)
    source = augment(jnp.concatenate([gap, skel[...], gap], 1), indicator, None)[0]
    source = [source[:, k * 256 : (k + 1) * 256].T for k in range(wide // 256)]
    gap = gap[:RHS_DEV]
    cof_high, cof_low = split(jnp.concatenate([gap, coeff[...], gap], 1))
    cof = jnp.concatenate([cof_high, cof_low], 0)
    for group in range(count // 4):
        lanes = slice(group * 256, (group + 1) * 256)
        around = slice(group * 256, group * 256 + 512)
        high, low = weights(mul(jnp.concatenate(source[group : group + 2], 0), target[:, lanes]))
        both = mul(cof[:, around], high)
        out[:, lanes] = both[:RHS_DEV] + both[RHS_DEV:] + mul(cof_high[:, around], low)


def down_kernel(
    gathered_any, roots_any, m0_any, s0_any, c0_any, lv1_any, lv2_any, root_any, basis_any, f1_any, f2_any, own_any,
    first_any, rest_any, out_any, f0, field0, field1, field2, gathered, roots, m0, s0, c0, lv1, lv2, root, basis, f1, f2,
    own_near, other_near, out, sems, out_sems,
):
    core = lax.axis_index("rhs")
    quarter = LANES // 4
    copies = fetch(
        [
            (roots_any, roots), (m0_any, m0), (s0_any, s0), (c0_any, c0), (gathered_any, gathered),
            (root_any, root), (f2_any, f2), (own_any, own_near),
            (first_any, other_near.at[:, pl.ds(0, CUT_AT)]),
            (rest_any, other_near.at[:, pl.ds(CUT_AT, NEAR_OUT - CUT_AT)]), (lv2_any, lv2), (f1_any, f1), (lv1_any, lv1), (basis_any, basis),
        ],
        sems,
    )
    for copy in copies:
        copy.start()

    for copy in copies[:4]:
        copy.wait()
    me = lax.axis_index("leaf")
    one = jnp.where(lax.broadcasted_iota(jnp.int32, (8, RANK), 0) == 0, 1.0, 0.0)
    pair = roots[:, pl.ds(pl.multiple_of((me // 2) * 128, 128), 128)]
    own = jnp.where(lax.broadcasted_iota(jnp.int32, (DIM, 128), 1) // RANK == lax.rem(me, 2), pair, 0.0)
    own_side = augment(own[:, :RANK] + own[:, RANK:], one, None)[0].T
    kernels = []
    for part in range(8):
        lanes = slice(part * 512, (part + 1) * 512)
        first = lax.broadcasted_iota(jnp.int32, (8, 512), 0) == 0
        cluster = part * 8 + lax.broadcasted_iota(jnp.int32, (8, 512), 1) // RANK
        penalty = jnp.where(first & (jnp.abs(cluster - me) < 2), CUT, 0.0)
        kernels.append(weights(mul(own_side, augment(roots[:, lanes], None, penalty)[1])))
    couple_level(m0, s0, c0, f0)

    for copy in copies[4:]:
        copy.wait()
    top = jnp.zeros((RHS_DEV, RANK), F32)
    for part, (high, low) in enumerate(kernels):
        pieces = []
        for chip in range(8 * part, 8 * part + 8):
            pieces.append(jnp.concatenate([gathered[chip, :, :RANK], gathered[chip, :, RANK:]], 0))
        cof_high, cof_low = split(jnp.concatenate(pieces, 1))
        both = mul(jnp.concatenate([cof_high, cof_low], 0), high, NT)
        top = top + both[:RHS_DEV] + both[RHS_DEV:] + mul(cof_high, low, NT)

    def coupled(ref, place):
        width = ref.shape[1]
        lanes = slice(LANES // 2 + place * EDGE, LANES // 2 + (place + 1) * EDGE)
        mine, theirs = own_near[:, lanes], other_near[:, lanes]
        ref[:, :EDGE] += jnp.where(core == 0, mine, theirs)
        ref[:, width - EDGE :] += jnp.where(core == 0, theirs, mine)

    coupled(f2, 2)
    field2[...] = f2[...] + mul3(top, root[...])

    def down_level(parents, transfer, coupled, children, count):
        for parent in range(count):
            lanes = slice(parent * 128, (parent + 1) * 128)
            above = parents[:, parent * RANK : (parent + 1) * RANK]
            children[:, lanes] = coupled[:, lanes] + mul3(above, transfer[:, lanes])

    coupled(f1, 1)
    down_level(field2, lv2, f1, field1, LEAVES_DEV // 4)
    coupled(f0, 0)
    down_level(field1, lv1, f0, field0, LEAVES_DEV // 2)

    stores = []
    for part in range(4):
        near, near_from = (own_near, other_near)[part // 2], part % 2 * quarter
        start = pl.multiple_of((core if part < 2 else 1 - core) * 2 * quarter + near_from, quarter)
        for pair in range(LEAVES_DEV // 8):
            fields = field0[:, pl.ds(pl.multiple_of(start // 4 + pair * 128, 128), 128)]
            for side in range(2):
                offset = (2 * pair + side) * LEAF
                lanes = pl.ds(pl.multiple_of(start + offset, LEAF), LEAF)
                far = mul3(fields[:, side * RANK : (side + 1) * RANK], basis[:, lanes])
                out[:, lanes] = near[:, near_from + offset : near_from + offset + LEAF] + far
        lanes = pl.ds(start, quarter)
        store = pltpu.make_async_copy(out.at[:, lanes], out_any.at[:, lanes], out_sems.at[part])
        store.start()
        stores.append(store)
    for store in stores:
        store.wait()


def shapes(*dims):
    return [jax.ShapeDtypeStruct(dim, F32) for dim in dims]


def cost(flops, bytes_accessed, transcendentals=0):
    return pl.CostEstimate(flops=flops, bytes_accessed=bytes_accessed, transcendentals=transcendentals)


SWAP = [(0, 1), (1, 0)]
NEAR_WAY = [pair for i in range(CHIPS - 1) for pair in ((2 * i, 2 * i + 2), (2 * i + 3, 2 * i + 1))]
CROSS_WAY = [pair for i in range(CHIPS - 1) for pair in ((2 * i + 1, 2 * i + 2), (2 * i + 2, 2 * i + 1))]


def call(kernel, outputs, inputs, scratch, estimate, name):
    def spec(place):
        return pl.BlockSpec(memory_space=place)

    several = isinstance(outputs, list)
    return pl.pallas_call(
        kernel,
        out_shape=outputs,
        in_specs=[spec(pl.ANY)] * len(inputs),
        out_specs=[spec(pl.ANY)] * len(outputs) if several else spec(pl.ANY),
        scratch_shapes=scratch,
        compiler_params=pltpu.CompilerParams(vmem_limit_bytes=64 * 2**20),
        cost_estimate=estimate,
        name=name,
    )(*inputs)


def vmem(*dims):
    return [pltpu.VMEM(dim, F32) for dim in dims]


def like(*arrays):
    return [pltpu.VMEM(array.shape, array.dtype) for array in arrays]


def dma_sems(count):
    return pltpu.SemaphoreType.DMA((count,))


def up_call(vec, basis, lv1, lv2, root, pts, s0, s1, s2):
    coeffs = ((RHS_DEV, 2048), (RHS_DEV, 1024), (RHS_DEV, 512))
    return call(
        up_kernel,
        shapes(*coeffs, (CHIPS, RHS_DEV // 2, 2 * RANK), (DIM, HALO + 5 * EDGE), (DIM, HALO + 2 * EDGE)),
        (vec, basis, lv1, lv2, root, pts, s0, s1, s2),
        like(vec, basis, lv1, lv2, root)
        + vmem(*coeffs, (CHIPS, RHS_DEV // 2, 2 * RANK), (DIM, HALO + 5 * EDGE), (DIM, HALO + 2 * EDGE))
        + [dma_sems(14), dma_sems(9)],
        cost(6 * 10**8, 6 * 10**6),
        "up",
    )


def near_call(mask, m0, m1, m2, s0, s1, s2, c1, c2, pts, vec, other_pts, other_vec, near_msg, cross_msg):
    return call(
        near_kernel,
        shapes((32, NEAR_OUT), (32, CUT_AT), (32, NEAR_OUT - CUT_AT), c1.shape, c2.shape),
        (mask, m0, m1, m2, s0, s1, s2, c1, c2, pts, vec, other_pts, other_vec, near_msg, cross_msg),
        vmem((32, NEAR_OUT), (32, NEAR_OUT))
        + like(c1, c2, m1, m2, s1, s2, c1, c2)
        + vmem((DIM, WINDOW * LEAF), (64, WINDOW * LEAF))
        + [
            pltpu.VMEM((WINDOW + 1, LEAF, 4 * DIM), BF16),
            pltpu.VMEM((HALF, 4 * DIM, LEAF), BF16),
            pltpu.VMEM((WINDOW + 1, 128, LEAF), BF16),
        ]
        + [pltpu.SMEM(array.shape, jnp.int32) for array in (mask, m0, m1, m2)]
        + vmem((DIM, 3 * EDGE), (DIM, 3 * EDGE), (DIM, 2 * EDGE), (DIM, 2 * EDGE))
        + [pltpu.SMEM((HALF * (2 * REACH + 1) + REST,), jnp.int32), dma_sems(24), dma_sems(5)],
        cost(10**10, 5 * 10**6, 5 * 10**6),
        "near",
    )


def down_call(gathered, roots, m0, s0, c0, lv1, lv2, root, basis, f1, f2, own_near, first, rest):
    inputs = (gathered, roots, m0, s0, c0, lv1, lv2, root, basis, f1, f2, own_near, first, rest)
    return call(
        down_kernel,
        jax.ShapeDtypeStruct((RHS_DEV, LANES), F32),
        inputs,
        like(c0, c0, f1, f2, *inputs[:-2], own_near) + vmem((RHS_DEV, LANES)) + [dma_sems(14), dma_sems(4)],
        cost(2 * 10**9, 8 * 10**6),
        "down",
    )


def per_device(
    points, vectors, leaf_basis, skel_lv0, skel_lv1, skel_lv2, transfer_lv1, transfer_lv2,
    transfer_root, root_skeleton_points, near_mask, far_lv0, far_lv1, far_lv2,
):
    pts, vec, basis = points.T, vectors.T, leaf_basis.T
    skels = (skel_lv0.T, skel_lv1.T, skel_lv2.T)
    lv1, lv2, root = transfer_lv1.T, transfer_lv2.T, transfer_root.T
    far = (far_lv0.T, far_lv1.T, far_lv2.T)
    both = ("leaf", "rhs")

    other_pts = lax.ppermute(pts, "rhs", SWAP)
    other_vec = lax.ppermute(vec, "rhs", SWAP)
    c0, c1, c2, blocks, near_msg, cross_msg = up_call(vec, basis, lv1, lv2, root, pts, *skels)
    near_msg = lax.ppermute(near_msg, both, NEAR_WAY)
    cross_msg = lax.ppermute(cross_msg, both, CROSS_WAY)
    gathered = lax.all_to_all(blocks, "leaf", split_axis=0, concat_axis=0, tiled=True)
    own_near, first, rest, f1, f2 = near_call(
        near_mask.T, *far, *skels, c1, c2, pts, vec, other_pts, other_vec, near_msg, cross_msg
    )
    first = lax.ppermute(first, "rhs", SWAP)
    rest = lax.ppermute(rest, "rhs", SWAP)
    return down_call(
        gathered, root_skeleton_points.T, far[0], skels[0], c0, lv1, lv2, root, basis, f1, f2, own_near, first, rest
    ).T


def solution(mesh):
    split_both = P("leaf", "rhs")
    placed = (split_both, split_both) + (P("leaf", None),) * 7 + (P(),) + (P("leaf", None),) * 4
    return jax.shard_map(per_device, mesh=mesh, in_specs=placed, out_specs=split_both, check_vma=False)
```

profile of v0, /device:TPU:1, one launch (start us, length us, event | category | flops | bytes accessed | tf_op | source)
XLA Modules:
  0.0 47.0 jit_solution(1482244366691258095)
XLA Ops:
  0.0 1.4 %collective-permute-start = (f32[32,8192]{1,0:T(8,128)}, f32[32,8192]{1,0:T(8,128)}, u32[]{:S(2)}, u32[]{:S(2)}) collective-permute-start(f32[32,8192]{1,0:T(8,128)} %bitcast.28), channel_id=1, source_target_pairs={{0,1},{1,0},{2,3},{3,2},{4,5},{5,4},{6,7},{7,6},{8,9},{9,8},{10,11... | collective-permute-start | bytes 3145736 | tf_op jit(solution)/shard_map/ppermute | solution.py:527
  1.4 0.0 collective-permute-start.1
  1.4 4.5 %up.1 = (f32[32,2048]{1,0:T(8,128)}, f32[32,1024]{1,0:T(8,128)}, f32[32,512]{1,0:T(8,128)}, f32[64,16,128]{2,1,0:T(8,128)}, f32[64,1664]{1,0:T(8,128)}, /*index=5*/f32[64,1280]{1,0:T(8,128)}) custom-call(f32[32,8192]{1,0:T(8,128)} %bitcast.26, f32[64,8192]{1,0:T(8,128)} %bitcast.15, f32[64,2048]{1,0:T(8,128)} %bitcast.17, f32[64,1024]{1,0:T(8,128)} %bitcast.23, ...), custom_call_target="tpu_custom_call" | custom-call | flops 600000000 | bytes 6000000 | tf_op jit(solution)/shard_map/up/pallas_call | solution.py:446
  5.9 1.3 %collective-permute-start.2 = (f32[64,1664]{1,0:T(8,128)}, f32[64,1664]{1,0:T(8,128)}, u32[]{:S(2)}, u32[]{:S(2)}) collective-permute-start(f32[64,1664]{1,0:T(8,128)} %get-tuple-element.20), channel_id=1, source_target_pairs={{0,2},{3,1},{2,4},{5,3},{4,6},{7,5},{6,8},{9,7},{8,10},{11,9},{10,... | collective-permute-start | bytes 1277960 | tf_op jit(solution)/shard_map/ppermute | solution.py:530
  7.2 6.6 %collective-permute-start.3 = (f32[64,1280]{1,0:T(8,128)}, f32[64,1280]{1,0:T(8,128)}, u32[]{:S(2)}, u32[]{:S(2)}) collective-permute-start(f32[64,1280]{1,0:T(8,128)} %get-tuple-element.21), channel_id=1, source_target_pairs={{1,2},{2,1},{3,4},{4,3},{5,6},{6,5},{7,8},{8,7},{9,10},{10,9},{11,... | collective-permute-start | bytes 983048 | tf_op jit(solution)/shard_map/ppermute | solution.py:531
  13.8 9.4 %all-to-all-start = ((f32[64,16,128]{2,1,0:T(8,128)}), f32[64,16,128]{2,1,0:T(8,128)}, u32[]{:S(2)}, u32[]{:S(2)}) async-start(f32[64,16,128]{2,1,0:T(8,128)} %get-tuple-element.16), calls=%async_computation | async-start | bytes 1048576 | tf_op jit(solution)/shard_map/all_to_all | solution.py:532
  23.2 0.0 collective-permute-done.3.cross_msg
  23.2 0.0 collective-permute-done.2.near_msg
  23.2 0.0 collective-permute-done.other_pts
  23.2 0.0 collective-permute-done.1.other_vec
  23.3 12.5 %near.1 = (f32[32,4480]{1,0:T(8,128)}, f32[32,2048]{1,0:T(8,128)}, f32[32,2432]{1,0:T(8,128)}, f32[32,1024]{1,0:T(8,128)}, f32[32,512]{1,0:T(8,128)}) custom-call(s32[8,32]{1,0:T(8,128)} %bitcast.39, s32[4,32]{1,0:T(4,128)} %bitcast.37, s32[4,16]{1,0:T(4,128)} %bitcast.40, s32[4,8]{1,0:T(4,128)} %bitcast.41, f32[64,2048]{1,0:T(8,128)} %bitcast.20, ...), custom_call_target="tpu_custom_call" | custom-call | flops 10000000000 | bytes 5000000 | tf_op jit(solution)/shard_map/near/pallas_call | solution.py:446
  35.8 2.2 %collective-permute-start.5 = (f32[32,2432]{1,0:T(8,128)}, f32[32,2432]{1,0:T(8,128)}, u32[]{:S(2)}, u32[]{:S(2)}) collective-permute-start(f32[32,2432]{1,0:T(8,128)} %get-tuple-element.26), channel_id=1, source_target_pairs={{0,1},{1,0},{2,3},{3,2},{4,5},{5,4},{6,7},{7,6},{8,9},{9,8},{10,11... | collective-permute-start | bytes 933896 | tf_op jit(solution)/shard_map/ppermute | solution.py:537
  38.0 0.3 collective-permute-start.4
  38.2 0.0 all-to-all-done.gathered_any
  38.2 1.7 %collective-permute-done.4.first_any = f32[32,2048]{1,0:T(8,128)} collective-permute-done((f32[32,2048]{1,0:T(8,128)}, f32[32,2048]{1,0:T(8,128)}, u32[]{:S(2)}, u32[]{:S(2)}) %collective-permute-start.4) | collective-permute-done | bytes 262176 | tf_op jit(solution)/shard_map/ppermute | solution.py:536
  39.9 0.0 collective-permute-done.5.rest_any
  39.9 6.9 %down.1 = f32[32,8192]{1,0:T(8,128)} custom-call(f32[64,16,128]{2,1,0:T(8,128)} %all-to-all-done.gathered_any, f32[64,4096]{1,0:T(8,128)} %bitcast.22, s32[4,32]{1,0:T(4,128)} %bitcast.38, f32[64,2048]{1,0:T(8,128)} %bitcast.21, f32[32,2048]{1,0:T(8,128)} %get-tuple-element.17.c0_any, f32[64,2048]{1,0:T(8,128)} %bitcast.18, f32[64,1024]{1,0:T(8,128)} %bitcast.24, ...), custom_call_target="tpu_custom_call" | custom-call | flops 2000000000 | bytes 8000000 | tf_op jit(solution)/shard_map/down/pallas_call | solution.py:446
Async XLA Ops:
  0.0 23.2 %collective-permute-start = (f32[32,8192]{1,0:T(8,128)}, f32[32,8192]{1,0:T(8,128)}, u32[]{:S(2)}, u32[]{:S(2)}) collective-permute-start(f32[32,8192]{1,0:T(8,128)} %bitcast.28), channel_id=1, source_target_pairs={{0,1},{1,0},{2,3},{3,2},{4,5},{5,4},{6,7},{7,6},{8,9},{9,8},{10,11... | collective-permute-start | bytes 3145736 | tf_op jit(solution)/shard_map/ppermute | solution.py:527
  1.4 21.8 %collective-permute-start.1 = (f32[32,8192]{1,0:T(8,128)}, f32[32,8192]{1,0:T(8,128)}, u32[]{:S(2)}, u32[]{:S(2)}) collective-permute-start(f32[32,8192]{1,0:T(8,128)} %bitcast.25), channel_id=1, source_target_pairs={{0,1},{1,0},{2,3},{3,2},{4,5},{5,4},{6,7},{7,6},{8,9},{9,8},{10,11... | collective-permute-start | bytes 3145736 | tf_op jit(solution)/shard_map/ppermute | solution.py:528
  5.9 17.3 %collective-permute-start.2 = (f32[64,1664]{1,0:T(8,128)}, f32[64,1664]{1,0:T(8,128)}, u32[]{:S(2)}, u32[]{:S(2)}) collective-permute-start(f32[64,1664]{1,0:T(8,128)} %get-tuple-element.20), channel_id=1, source_target_pairs={{0,2},{3,1},{2,4},{5,3},{4,6},{7,5},{6,8},{9,7},{8,10},{11,9},{10,... | collective-permute-start | bytes 1277960 | tf_op jit(solution)/shard_map/ppermute | solution.py:530
  7.2 16.0 %collective-permute-start.3 = (f32[64,1280]{1,0:T(8,128)}, f32[64,1280]{1,0:T(8,128)}, u32[]{:S(2)}, u32[]{:S(2)}) collective-permute-start(f32[64,1280]{1,0:T(8,128)} %get-tuple-element.21), channel_id=1, source_target_pairs={{1,2},{2,1},{3,4},{4,3},{5,6},{6,5},{7,8},{8,7},{9,10},{10,9},{11,... | collective-permute-start | bytes 983048 | tf_op jit(solution)/shard_map/ppermute | solution.py:531
  13.8 24.5 %all-to-all-start = ((f32[64,16,128]{2,1,0:T(8,128)}), f32[64,16,128]{2,1,0:T(8,128)}, u32[]{:S(2)}, u32[]{:S(2)}) async-start(f32[64,16,128]{2,1,0:T(8,128)} %get-tuple-element.16), calls=%async_computation | async-start | bytes 1048576 | tf_op jit(solution)/shard_map/all_to_all | solution.py:532
  35.8 4.1 %collective-permute-start.5 = (f32[32,2432]{1,0:T(8,128)}, f32[32,2432]{1,0:T(8,128)}, u32[]{:S(2)}, u32[]{:S(2)}) collective-permute-start(f32[32,2432]{1,0:T(8,128)} %get-tuple-element.26), channel_id=1, source_target_pairs={{0,1},{1,0},{2,3},{3,2},{4,5},{5,4},{6,7},{7,6},{8,9},{9,8},{10,11... | collective-permute-start | bytes 933896 | tf_op jit(solution)/shard_map/ppermute | solution.py:537
  38.0 1.9 %collective-permute-start.4 = (f32[32,2048]{1,0:T(8,128)}, f32[32,2048]{1,0:T(8,128)}, u32[]{:S(2)}, u32[]{:S(2)}) collective-permute-start(f32[32,2048]{1,0:T(8,128)} %get-tuple-element.25), channel_id=1, source_target_pairs={{0,1},{1,0},{2,3},{3,2},{4,5},{5,4},{6,7},{7,6},{8,9},{9,8},{10,11... | collective-permute-start | bytes 786440 | tf_op jit(solution)/shard_map/ppermute | solution.py:536
where the time goes:
time: 46.8 us; the launch traced here: 47 us
  Pallas kernels  23.9 us (51%)
  starting transfers between devices  21.1 us (45%)
  waiting for transfers between devices  1.69 us (4%)
    pallas_call x3, Pallas kernels, call(): pl.pallas_call(kernel, out_shape=outputs, in_specs=[spec(pl.ANY)] * len(i...  23.9 us
    all_to_all x1, starting transfers between devices, per_device(): lax.all_to_all(blocks, 'leaf', split_axis=0, concat_axis=0, tiled=True)  9.41 us
    ppermute x1, starting transfers between devices, per_device(): cross_msg = lax.ppermute(cross_msg, both, CROSS_WAY)  6.56 us
    ppermute x1, starting transfers between devices, per_device(): rest = lax.ppermute(rest, 'rhs', SWAP)  2.19 us
    ppermute x1, waiting for transfers between devices, per_device(): first = lax.ppermute(first, 'rhs', SWAP)  1.67 us
    ppermute x1, starting transfers between devices, per_device(): other_pts = lax.ppermute(pts, 'rhs', SWAP)  1.42 us
    ppermute x1, starting transfers between devices, per_device(): near_msg = lax.ppermute(near_msg, both, NEAR_WAY)  1.29 us
  transfers between devices with their start and end apart: 7, of which 1 were waited for; matrix products, arithmetic and copies ran while one was open for 0% of the time, Pallas kernels for 36%

commit v1 on v0

--- a/solution.py
+++ b/solution.py
@@ -50,6 +50,25 @@
     right_high, right_low = split(right)
     both = mul(jnp.concatenate([left_high, left_low], 0), right_high, dims)
     return both[:rows] + both[rows:] + mul(left_high, right_low, dims)
+
+
+def low_lanes(rows):
+    return lax.broadcasted_iota(jnp.int32, (rows, 2 * RANK), 1) < RANK
+
+
+def stack(x):
+    return jnp.concatenate(split(x), 0)
+
+
+def pair_products(pair, rights):
+    turned = pltpu.roll(pair, RANK, 1)
+    rows = pair.shape[0]
+    low = low_lanes(rows)
+    out = []
+    for left, right in zip((jnp.where(low, pair, turned), jnp.where(low, turned, pair)), rights):
+        both = mul(stack(left), stack(right))
+        out.append(both[:rows] + both[rows:])
+    return out
 
 
 def augment(points, source_extra=None, target_extra=None):
@@ -297,16 +316,18 @@
 
         lax.fori_loop(0, number, step, 0)
 
-    full = count // GROUP
-    steps(0, GROUP, full)
-    steps(full * GROUP, REST, (count - full * GROUP + REST - 1) // REST)
+    done = jnp.int32(0)
+    for size in (GROUP, GROUP // 2, REST):
+        number = (count - done + REST - 1) // size
+        steps(done, size, number)
+        done = done + number * size
     for store in stores[2:]:
         store.start()
     for store in stores:
         store.wait()
 
 
-def couple_level(mask, skel, coeff, out):
+def couple_level(mask, skel, coeff, out, beside=None):
     width = skel.shape[1]
     count = width // RANK
     cluster = lax.broadcasted_iota(jnp.int32, (count, width), 0)
@@ -337,6 +358,8 @@
         high, low = weights(mul(jnp.concatenate(source[group : group + 2], 0), target[:, lanes]))
         both = mul(cof[:, around], high)
         out[:, lanes] = both[:RHS_DEV] + both[RHS_DEV:] + mul(cof_high[:, around], low)
+        if beside is not None:
+            beside(group)
 
 
 def down_kernel(
@@ -346,12 +369,17 @@
 ):
     core = lax.axis_index("rhs")
     quarter = LANES // 4
+    body, ends = pl.ds(0, HALF * LEAF), pl.ds(HALF * LEAF, 3 * EDGE)
+    late = pl.ds(HALF * LEAF - CUT_AT, 3 * EDGE)
+    second, rest_body = pl.ds(CUT_AT, HALF * LEAF - CUT_AT), pl.ds(0, HALF * LEAF - CUT_AT)
     copies = fetch(
         [
-            (roots_any, roots), (m0_any, m0), (s0_any, s0), (c0_any, c0), (gathered_any, gathered),
-            (root_any, root), (f2_any, f2), (own_any, own_near),
+            (roots_any, roots), (m0_any, m0), (s0_any, s0), (c0_any, c0),
+            (gathered_any, gathered), (root_any, root), (f2_any, f2), (lv2_any, lv2), (f1_any, f1), (lv1_any, lv1),
+            (own_any.at[:, ends], own_near.at[:, ends]), (rest_any.at[:, late], other_near.at[:, ends]),
+            (basis_any, basis), (own_any.at[:, body], own_near.at[:, body]),
             (first_any, other_near.at[:, pl.ds(0, CUT_AT)]),
-            (rest_any, other_near.at[:, pl.ds(CUT_AT, NEAR_OUT - CUT_AT)]), (lv2_any, lv2), (f1_any, f1), (lv1_any, lv1), (basis_any, basis),
+            (rest_any.at[:, rest_body], other_near.at[:, second]),
         ],
         sems,
     )
@@ -366,13 +394,15 @@
     own = jnp.where(lax.broadcasted_iota(jnp.int32, (DIM, 128), 1) // RANK == lax.rem(me, 2), pair, 0.0)
     own_side = augment(own[:, :RANK] + own[:, RANK:], one, None)[0].T
     kernels = []
-    for part in range(8):
+
+    def root_part(part):
         lanes = slice(part * 512, (part + 1) * 512)
         first = lax.broadcasted_iota(jnp.int32, (8, 512), 0) == 0
         cluster = part * 8 + lax.broadcasted_iota(jnp.int32, (8, 512), 1) // RANK
         penalty = jnp.where(first & (jnp.abs(cluster - me) < 2), CUT, 0.0)
         kernels.append(weights(mul(own_side, augment(roots[:, lanes], None, penalty)[1])))
-    couple_level(m0, s0, c0, f0)
+
+    couple_level(m0, s0, c0, f0, root_part)
 
     for copy in copies[4:]:
         copy.wait()
@@ -396,10 +426,11 @@
     field2[...] = f2[...] + mul3(top, root[...])
 
     def down_level(parents, transfer, coupled, children, count):
-        for parent in range(count):
-            lanes = slice(parent * 128, (parent + 1) * 128)
-            above = parents[:, parent * RANK : (parent + 1) * RANK]
-            children[:, lanes] = coupled[:, lanes] + mul3(above, transfer[:, lanes])
+        for pair in range(count // 2):
+            lanes = [slice((2 * pair + side) * 128, (2 * pair + side + 1) * 128) for side in range(2)]
+            above = parents[:, pair * 128 : (pair + 1) * 128]
+            for at, below in zip(lanes, pair_products(above, [transfer[:, at] for at in lanes])):
+                children[:, at] = coupled[:, at] + below
 
     coupled(f1, 1)
     down_level(field2, lv2, f1, field1, LEAVES_DEV // 4)
@@ -412,11 +443,10 @@
         start = pl.multiple_of((core if part < 2 else 1 - core) * 2 * quarter + near_from, quarter)
         for pair in range(LEAVES_DEV // 8):
             fields = field0[:, pl.ds(pl.multiple_of(start // 4 + pair * 128, 128), 128)]
-            for side in range(2):
-                offset = (2 * pair + side) * LEAF
-                lanes = pl.ds(pl.multiple_of(start + offset, LEAF), LEAF)
-                far = mul3(fields[:, side * RANK : (side + 1) * RANK], basis[:, lanes])
-                out[:, lanes] = near[:, near_from + offset : near_from + offset + LEAF] + far
+            offsets = [(2 * pair + side) * LEAF for side in range(2)]
+            lanes = [pl.ds(pl.multiple_of(start + offset, LEAF), LEAF) for offset in offsets]
+            for offset, at, far in zip(offsets, lanes, pair_products(fields, [basis[:, at] for at in lanes])):
+                out[:, at] = near[:, near_from + offset : near_from + offset + LEAF] + far
         lanes = pl.ds(start, quarter)
         store = pltpu.make_async_copy(out.at[:, lanes], out_any.at[:, lanes], out_sems.at[part])
         store.start()
@@ -508,7 +538,7 @@
         down_kernel,
         jax.ShapeDtypeStruct((RHS_DEV, LANES), F32),
         inputs,
-        like(c0, c0, f1, f2, *inputs[:-2], own_near) + vmem((RHS_DEV, LANES)) + [dma_sems(14), dma_sems(4)],
+        like(c0, c0, f1, f2, *inputs[:-2], own_near) + vmem((RHS_DEV, LANES)) + [dma_sems(16), dma_sems(4)],
         cost(2 * 10**9, 8 * 10**6),
         "down",
     )

time: 46.8 us -> 46.1 us (0.985); the launches traced: 47 us -> 45.6 us
  Pallas kernels: 23.9 us -> 22 us
  starting transfers between devices: 21.1 us -> 21.8 us
    pallas_call x3, Pallas kernels: 23.9 us -> 22 us  [call(): pl.pallas_call(kernel, out_shape=outputs, in_specs=[spec(pl.ANY)] * len(i...]
    ppermute x1, starting transfers between devices: 2.19 us -> 2.8 us  [per_device(): rest = lax.ppermute(rest, 'rhs', SWAP)]
  transfers between devices with their start and end apart: 7 -> 7, of which waited for: 1 -> 1; matrix products, arithmetic and copies ran while one was open for 0% -> 0% of each run, Pallas kernels for 36% -> 33%
where the time goes in v1:
time: 46.1 us; the launch traced here: 45.6 us
  Pallas kernels  22 us (48%)
  starting transfers between devices  21.8 us (47%)
  waiting for transfers between devices  1.69 us (4%)
    pallas_call x3, Pallas kernels, call(): pl.pallas_call(kernel, out_shape=outputs, in_specs=[spec(pl.ANY)] * len(i...  22 us
    all_to_all x1, starting transfers between devices, per_device(): lax.all_to_all(blocks, 'leaf', split_axis=0, concat_axis=0, tiled=True)  9.41 us
    ppermute x1, starting transfers between devices, per_device(): cross_msg = lax.ppermute(cross_msg, both, CROSS_WAY)  6.56 us
    ppermute x1, starting transfers between devices, per_device(): rest = lax.ppermute(rest, 'rhs', SWAP)  2.8 us
    ppermute x1, waiting for transfers between devices, per_device(): first = lax.ppermute(first, 'rhs', SWAP)  1.67 us
    ppermute x1, starting transfers between devices, per_device(): other_pts = lax.ppermute(pts, 'rhs', SWAP)  1.42 us
    ppermute x1, starting transfers between devices, per_device(): near_msg = lax.ppermute(near_msg, both, NEAR_WAY)  1.29 us
  transfers between devices with their start and end apart: 7, of which 1 were waited for; matrix products, arithmetic and copies ran while one was open for 0% of the time, Pallas kernels for 33%

profile of v1, /device:TPU:1, one launch (start us, length us, event | category | flops | bytes accessed | tf_op | source)
XLA Modules:
  0.0 45.6 jit_solution(4915857275071467645)
XLA Ops:
  0.0 1.4 %collective-permute-start = (f32[32,8192]{1,0:T(8,128)}, f32[32,8192]{1,0:T(8,128)}, u32[]{:S(2)}, u32[]{:S(2)}) collective-permute-start(f32[32,8192]{1,0:T(8,128)} %bitcast.28), channel_id=1, source_target_pairs={{0,1},{1,0},{2,3},{3,2},{4,5},{5,4},{6,7},{7,6},{8,9},{9,8},{10,11... | collective-permute-start | bytes 3145736 | tf_op jit(solution)/shard_map/ppermute | solution.py:557
  1.4 0.0 collective-permute-start.1
  1.4 4.5 %up.1 = (f32[32,2048]{1,0:T(8,128)}, f32[32,1024]{1,0:T(8,128)}, f32[32,512]{1,0:T(8,128)}, f32[64,16,128]{2,1,0:T(8,128)}, f32[64,1664]{1,0:T(8,128)}, /*index=5*/f32[64,1280]{1,0:T(8,128)}) custom-call(f32[32,8192]{1,0:T(8,128)} %bitcast.26, f32[64,8192]{1,0:T(8,128)} %bitcast.15, f32[64,2048]{1,0:T(8,128)} %bitcast.17, f32[64,1024]{1,0:T(8,128)} %bitcast.23, ...), custom_call_target="tpu_custom_call" | custom-call | flops 600000000 | bytes 6000000 | tf_op jit(solution)/shard_map/up/pallas_call | solution.py:476
  5.9 1.3 %collective-permute-start.2 = (f32[64,1664]{1,0:T(8,128)}, f32[64,1664]{1,0:T(8,128)}, u32[]{:S(2)}, u32[]{:S(2)}) collective-permute-start(f32[64,1664]{1,0:T(8,128)} %get-tuple-element.20), channel_id=1, source_target_pairs={{0,2},{3,1},{2,4},{5,3},{4,6},{7,5},{6,8},{9,7},{8,10},{11,9},{10,... | collective-permute-start | bytes 1277960 | tf_op jit(solution)/shard_map/ppermute | solution.py:560
  7.2 6.6 %collective-permute-start.3 = (f32[64,1280]{1,0:T(8,128)}, f32[64,1280]{1,0:T(8,128)}, u32[]{:S(2)}, u32[]{:S(2)}) collective-permute-start(f32[64,1280]{1,0:T(8,128)} %get-tuple-element.21), channel_id=1, source_target_pairs={{1,2},{2,1},{3,4},{4,3},{5,6},{6,5},{7,8},{8,7},{9,10},{10,9},{11,... | collective-permute-start | bytes 983048 | tf_op jit(solution)/shard_map/ppermute | solution.py:561
  13.8 9.4 %all-to-all-start = ((f32[64,16,128]{2,1,0:T(8,128)}), f32[64,16,128]{2,1,0:T(8,128)}, u32[]{:S(2)}, u32[]{:S(2)}) async-start(f32[64,16,128]{2,1,0:T(8,128)} %get-tuple-element.16), calls=%async_computation | async-start | bytes 1048576 | tf_op jit(solution)/shard_map/all_to_all | solution.py:562
  23.2 0.0 collective-permute-done.3.cross_msg
  23.2 0.0 collective-permute-done.2.near_msg
  23.2 0.0 collective-permute-done.other_pts
  23.2 0.0 collective-permute-done.1.other_vec
  23.3 10.7 %near.1 = (f32[32,4480]{1,0:T(8,128)}, f32[32,2048]{1,0:T(8,128)}, f32[32,2432]{1,0:T(8,128)}, f32[32,1024]{1,0:T(8,128)}, f32[32,512]{1,0:T(8,128)}) custom-call(s32[8,32]{1,0:T(8,128)} %bitcast.39, s32[4,32]{1,0:T(4,128)} %bitcast.37, s32[4,16]{1,0:T(4,128)} %bitcast.40, s32[4,8]{1,0:T(4,128)} %bitcast.41, f32[64,2048]{1,0:T(8,128)} %bitcast.20, ...), custom_call_target="tpu_custom_call" | custom-call | flops 10000000000 | bytes 5000000 | tf_op jit(solution)/shard_map/near/pallas_call | solution.py:476
  34.0 2.8 %collective-permute-start.5 = (f32[32,2432]{1,0:T(8,128)}, f32[32,2432]{1,0:T(8,128)}, u32[]{:S(2)}, u32[]{:S(2)}) collective-permute-start(f32[32,2432]{1,0:T(8,128)} %get-tuple-element.26), channel_id=1, source_target_pairs={{0,1},{1,0},{2,3},{3,2},{4,5},{5,4},{6,7},{7,6},{8,9},{9,8},{10,11... | collective-permute-start | bytes 933896 | tf_op jit(solution)/shard_map/ppermute | solution.py:567
  36.8 0.3 collective-permute-start.4
  37.1 0.0 all-to-all-done.gathered_any
  37.1 1.7 %collective-permute-done.4.first_any = f32[32,2048]{1,0:T(8,128)} collective-permute-done((f32[32,2048]{1,0:T(8,128)}, f32[32,2048]{1,0:T(8,128)}, u32[]{:S(2)}, u32[]{:S(2)}) %collective-permute-start.4) | collective-permute-done | bytes 262176 | tf_op jit(solution)/shard_map/ppermute | solution.py:566
  38.7 0.0 collective-permute-done.5.rest_any
  38.7 6.7 %down.1 = f32[32,8192]{1,0:T(8,128)} custom-call(f32[64,16,128]{2,1,0:T(8,128)} %all-to-all-done.gathered_any, f32[64,4096]{1,0:T(8,128)} %bitcast.22, s32[4,32]{1,0:T(4,128)} %bitcast.38, f32[64,2048]{1,0:T(8,128)} %bitcast.21, f32[32,2048]{1,0:T(8,128)} %get-tuple-element.17.c0_any, f32[64,2048]{1,0:T(8,128)} %bitcast.18, f32[64,1024]{1,0:T(8,128)} %bitcast.24, ...), custom_call_target="tpu_custom_call" | custom-call | flops 2000000000 | bytes 8000000 | tf_op jit(solution)/shard_map/down/pallas_call | solution.py:476
Async XLA Ops:
  0.0 23.2 %collective-permute-start = (f32[32,8192]{1,0:T(8,128)}, f32[32,8192]{1,0:T(8,128)}, u32[]{:S(2)}, u32[]{:S(2)}) collective-permute-start(f32[32,8192]{1,0:T(8,128)} %bitcast.28), channel_id=1, source_target_pairs={{0,1},{1,0},{2,3},{3,2},{4,5},{5,4},{6,7},{7,6},{8,9},{9,8},{10,11... | collective-permute-start | bytes 3145736 | tf_op jit(solution)/shard_map/ppermute | solution.py:557
  1.4 21.8 %collective-permute-start.1 = (f32[32,8192]{1,0:T(8,128)}, f32[32,8192]{1,0:T(8,128)}, u32[]{:S(2)}, u32[]{:S(2)}) collective-permute-start(f32[32,8192]{1,0:T(8,128)} %bitcast.25), channel_id=1, source_target_pairs={{0,1},{1,0},{2,3},{3,2},{4,5},{5,4},{6,7},{7,6},{8,9},{9,8},{10,11... | collective-permute-start | bytes 3145736 | tf_op jit(solution)/shard_map/ppermute | solution.py:558
  5.9 17.3 %collective-permute-start.2 = (f32[64,1664]{1,0:T(8,128)}, f32[64,1664]{1,0:T(8,128)}, u32[]{:S(2)}, u32[]{:S(2)}) collective-permute-start(f32[64,1664]{1,0:T(8,128)} %get-tuple-element.20), channel_id=1, source_target_pairs={{0,2},{3,1},{2,4},{5,3},{4,6},{7,5},{6,8},{9,7},{8,10},{11,9},{10,... | collective-permute-start | bytes 1277960 | tf_op jit(solution)/shard_map/ppermute | solution.py:560
  7.2 16.0 %collective-permute-start.3 = (f32[64,1280]{1,0:T(8,128)}, f32[64,1280]{1,0:T(8,128)}, u32[]{:S(2)}, u32[]{:S(2)}) collective-permute-start(f32[64,1280]{1,0:T(8,128)} %get-tuple-element.21), channel_id=1, source_target_pairs={{1,2},{2,1},{3,4},{4,3},{5,6},{6,5},{7,8},{8,7},{9,10},{10,9},{11,... | collective-permute-start | bytes 983048 | tf_op jit(solution)/shard_map/ppermute | solution.py:561
  13.8 23.3 %all-to-all-start = ((f32[64,16,128]{2,1,0:T(8,128)}), f32[64,16,128]{2,1,0:T(8,128)}, u32[]{:S(2)}, u32[]{:S(2)}) async-start(f32[64,16,128]{2,1,0:T(8,128)} %get-tuple-element.16), calls=%async_computation | async-start | bytes 1048576 | tf_op jit(solution)/shard_map/all_to_all | solution.py:562
  34.0 4.8 %collective-permute-start.5 = (f32[32,2432]{1,0:T(8,128)}, f32[32,2432]{1,0:T(8,128)}, u32[]{:S(2)}, u32[]{:S(2)}) collective-permute-start(f32[32,2432]{1,0:T(8,128)} %get-tuple-element.26), channel_id=1, source_target_pairs={{0,1},{1,0},{2,3},{3,2},{4,5},{5,4},{6,7},{7,6},{8,9},{9,8},{10,11... | collective-permute-start | bytes 933896 | tf_op jit(solution)/shard_map/ppermute | solution.py:567
  36.8 1.9 %collective-permute-start.4 = (f32[32,2048]{1,0:T(8,128)}, f32[32,2048]{1,0:T(8,128)}, u32[]{:S(2)}, u32[]{:S(2)}) collective-permute-start(f32[32,2048]{1,0:T(8,128)} %get-tuple-element.25), channel_id=1, source_target_pairs={{0,1},{1,0},{2,3},{3,2},{4,5},{5,4},{6,7},{7,6},{8,9},{9,8},{10,11... | collective-permute-start | bytes 786440 | tf_op jit(solution)/shard_map/ppermute | solution.py:566
